TPU v7x, 32 devices: a whole 2x2x4 slice. The times are simulated.
32 devices in a mesh: groups: 2 (over y), seq: 4 (over z), head: 2 (over x), section: 2 (over core).
Axes of the slice: x: 2, y: 2, z: 4, core: 2. Of those that a mesh axis runs over, the one named last changes fastest.
Arguments:
- q_heads: bfloat16 [2, 1024, 12288], P('section', ('groups', 'seq'), 'head'), parts along dimension 1, may hold values from -256 to 256
- cache_latent: bfloat16 [2, 1024, 512], P('section', ('groups', 'seq')), parts along dimension 1, may hold values from -6 to 6
- cache_rope: bfloat16 [2, 1024, 64], P('section', ('groups', 'seq')), parts along dimension 1, may hold values from -6.5 to 6.5
- span_start: int32 [2, 4], P('section', 'groups'), parts along dimension 1, may hold values from 1 to 256, as said below
- prefix_len: int32 [2, 4], P('section', 'groups'), parts along dimension 1, may hold values from 0 to 256, as said below
- key_up: bfloat16 [2, 64, 128, 512], P('section', 'head'), may hold values from -0.5 to 0.5
- value_up: bfloat16 [2, 64, 512, 128], P('section', 'head'), may hold values from -2 to 2
- out_weight: bfloat16 [2, 8192, 7168], P('section', 'head', 'seq'), may hold values from -0.0625 to 0.0625
Outputs:
- mixed_out: bfloat16 [2, 1024, 7168], P('section', ('groups', 'head'), 'seq'), parts along dimension 1
There are 2 independent parts, one for each index of `groups`. A program takes and returns all parts, laid end to end along the dimension named above; an argument that names none is the same for every part. Nothing has to cross between parts.
Inputs may be any that keep to these rules, and one draw needn't show every extreme that they name: Span j's own tokens are context positions span_start to span_start + 255; the last span of every layer starts at 256. `prefix_len`: below the span's span_start for every span but the last; equal to it for the last span of every layer.
All inputs are finite; a program needn't handle non-finite values.
Results may differ from a plain program's by a relative error of at most 0.0085.
Values may be sent and summed in bfloat16 or wider, within the bound.
A program may use at most 64 MiB of HBM per device.

v0:
```python
import jax
import jax.numpy as jnp
from jax import lax
from jax.sharding import PartitionSpec as P

NSPAN = 2


masked_fill = -1e30


def on_device(
    q_heads, cache_latent, cache_rope, span_start, prefix_len, key_up, value_up, out_weight
):
    queries_flat = q_heads[0]
    tokens = queries_flat.shape[0]
    head_count = key_up.shape[1]
    nope_dim = key_up.shape[2]
    head_width = queries_flat.shape[1] // head_count
    seq_count = lax.axis_size("seq")
    seq_index = lax.axis_index("seq")
    queries = queries_flat.reshape(tokens, head_count, head_width)
    absorbed = jnp.einsum(
        "thn,hnl->thl", queries[:, :, :nope_dim], key_up[0], preferred_element_type=jnp.float32
    ).astype(jnp.bfloat16)
    rope_query = queries[:, :, nope_dim:]
    softmax_scale = head_width ** (-0.5)
    span_len = tokens * seq_count // NSPAN
    global_row = seq_index * tokens + jnp.arange(tokens, dtype=jnp.int32)
    one_hot = (global_row // span_len)[:, None] == jnp.arange(NSPAN, dtype=jnp.int32)[None, :]
    span_first = jnp.sum(jnp.where(one_hot, span_start[0][None, :], 0), axis=1)
    prefix_row = jnp.sum(jnp.where(one_hot, prefix_len[0][None, :], 0), axis=1)
    token_pos = span_first + global_row % span_len
    local_latent = cache_latent[0]
    local_rope = cache_rope[0]
    lat_piece = lax.all_gather(local_latent, "seq", axis=0, tiled=True)
    running = jnp.full((tokens, head_count), masked_fill, jnp.float32)
    key_pos = jnp.arange(lat_piece.shape[0], dtype=jnp.int32)
    visible = (
        (key_pos[None, :] < prefix_row[:, None])
        | (key_pos[None, :] >= span_first[:, None]) & (key_pos[None, :] <= token_pos[:, None])
    )[:, None, :]
    scores = jnp.einsum(
        "thl,kl->thk", absorbed, lat_piece, preferred_element_type=jnp.float32
    ) + jnp.einsum(
        "thr,kr->thk",
        rope_query,
        lax.all_gather(local_rope, "seq", axis=0, tiled=True),
        preferred_element_type=jnp.float32,
    )
    scores = jnp.where(visible, scores * softmax_scale, masked_fill)
    new_max = jnp.maximum(running, jnp.max(scores, axis=2))
    weights = jnp.where(visible, jnp.exp(scores - new_max[:, :, None]), 0.0)
    totals = jnp.sum(weights, axis=2)
    summed = jnp.einsum(
        "thk,kl->thl", weights.astype(jnp.bfloat16), lat_piece, preferred_element_type=jnp.float32
    )
    final_state = (new_max, totals, summed)
    running, totals, summed = final_state
    latent_out = (summed / totals[:, :, None]).astype(jnp.bfloat16)
    head_out = (
        jnp.einsum("thl,hlv->thv", latent_out, value_up[0], preferred_element_type=jnp.float32)
        .astype(jnp.bfloat16)
        .reshape(tokens, -1)
    )
    partial_out = jnp.dot(
        lax.all_gather(head_out, "seq", axis=0, tiled=True),
        out_weight[0],
        preferred_element_type=jnp.float32,
    )
    mixed_out = lax.psum_scatter(partial_out, "head", scatter_dimension=0, tiled=True).astype(
        jnp.bfloat16
    )
    return mixed_out[None]


def solution(mesh):
    in_specs = (
        P("section", ("groups", "seq"), "head"),
        P("section", ("groups", "seq"), None),
        P("section", ("groups", "seq"), None),
        P("section", "groups"),
        P("section", "groups"),
        P("section", "head", None, None),
        P("section", "head", None, None),
        P("section", "head", "seq"),
    )
    out_specs = P("section", ("groups", "head"), "seq")
    return jax.shard_map(
        on_device, mesh=mesh, in_specs=in_specs, out_specs=out_specs, check_vma=False
    )
```

profile of v0, /device:TPU:0, one launch (start us, length us, event | category | flops | bytes accessed | tf_op | source)
XLA Modules:
  0.0 218.4 jit_solution(14006893475179986472)
XLA Ops:
  6.5 0.0 all-gather.4.cloned.1.call-start
  6.5 0.8 select_reduce_fusion.1
  7.3 13.9 %all-gather.1 = bf16[1,512,64]{1,2,0:T(8,128)(2,1)S(1)} all-gather(bf16[1,128,64]{1,2,0:T(8,128)(2,1)} %param.10), channel_id=3, replica_groups=mesh['groups'=2,'seq'=4,'head'=2,'section'=2] {'seq'}, dimensions={1}, use_global_device_ids=true | all-gather | bytes 81920 | tf_op jit(solution)/shard_map/all_gather | solution.py:48
  21.2 16.1 %all-gather = bf16[1,512,512]{2,1,0:T(8,128)(2,1)S(1)} all-gather(bf16[1,128,512]{2,1,0:T(8,128)(2,1)} %param.9), channel_id=2, replica_groups=mesh['groups'=2,'seq'=4,'head'=2,'section'=2] {'seq'}, dimensions={1}, use_global_device_ids=true | all-gather | bytes 655360 | tf_op jit(solution)/shard_map/all_gather | solution.py:36
  37.3 1.9 copy.11
  39.2 0.2 fusion.35
  39.4 8.9 %fusion.8 = f32[128,32,512]{2,0,1:T(8,128)} fusion(bf16[1,32,128,512]{3,2,1,0:T(8,128)(2,1)} %param.13, bf16[128,32,192]{0,2,1:T(8,128)(2,1)S(1)} %bitcast.40, bf16[1,512,512]{2,1,0:T(8,128)(2,1)S(1)} %all-gather), kind=kOutput, calls=%fused_computation.10 | convolution fusion | flops 2686451712 | bytes 14155776 | tf_op jit(solution)/shard_map/thl,kl->thk/dot_general | solution.py:43
  48.3 5.2 %fusion.41 = (f32[128,32]{0,1:T(8,128)S(1)}, f32[128,32,512]{2,0,1:T(8,128)S(1)}) fusion(f32[128,32,512]{2,0,1:T(8,128)} %fusion.8, bf16[1,512,64]{1,2,0:T(8,128)(2,1)S(1)} %all-gather.1, bf16[128,32,192]{0,2,1:T(8,128)(2,1)S(1)} %bitcast.41, pred[128,512]{1,0:T(8,128)(4,1)S(1)} %fusion.35), kind=kOutput, calls=%fused_computation.42 | convolution fusion | flops 276819968 | bytes 17448960 | tf_op jit(solution)/shard_map/thr,kr->thk/dot_general | solution.py:45
  53.5 0.0 copy-start
  53.6 3.2 %copy-done = f32[128,32,512]{2,0,1:T(8,128)} copy-done((f32[128,32,512]{2,0,1:T(8,128)}, f32[128,32,512]{2,0,1:T(8,128)S(1)}, u32[]{:S(2)}) %copy-start) | copy-done | bytes 8388632
  56.8 2.4 %fusion.2 = f32[128,32]{0,1:T(8,128)S(1)} fusion(f32[128,32,512]{2,0,1:T(8,128)S(1)} %get-tuple-element.8, f32[128,32]{0,1:T(8,128)S(1)} %broadcast_maximum_fusion, pred[128,512]{1,0:T(8,128)(4,1)S(1)} %fusion.35), kind=kLoop, calls=%fused_computation.5 | loop fusion | flops 6287360 | bytes 8486912 | tf_op jit(solution)/shard_map/reduce_sum | solution.py:54
  59.2 8.0 %fusion.24 = bf16[32,128,128]{1,2,0:T(8,128)(2,1)} fusion(bf16[1,32,512,128]{3,2,1,0:T(8,128)(2,1)} %param.14, f32[128,32]{0,1:T(8,128)S(1)} %fusion.2, f32[128,32,512]{2,0,1:T(8,128)} %copy-done, f32[128,32]{0,1:T(8,128)S(1)} %broadcast_maximum_fusion, pred[128,512]{1,0:T(8,128)(4,1)S(1)} %fusion.35, bf16[1,512,512]{2,1,0:T(8,128)(2,1)S(1)} %all-gather), kind=kOutput, calls=%fused_computation.18 | convolution fusion | flops 2695364608 | bytes 14254080 | tf_op jit(solution)/shard_map/thl,hlv->thv/dot_general | solution.py:62
  67.2 0.0 all-gather.4.cloned.1.call-update
  67.2 0.0 reduce-scatter.2.cloned.1.call-start
  67.2 79.7 %all-gather.4.cloned.1.call-done = bf16[512,4096]{0,1:T(8,128)(2,1)} async-done(((bf16[128,4096]{0,1:T(8,128)(2,1)}), bf16[512,4096]{0,1:T(8,128)(2,1)}) %all-gather.4.cloned.1.call-update) | async-done | bytes 4194320 | tf_op jit(solution)/shard_map/all_gather | solution.py:67
  147.0 14.6 %fusion = f32[512,1792]{1,0:T(8,128)} fusion(bf16[512,4096]{0,1:T(8,128)(2,1)} %all-gather.4.cloned.1.call-done, bf16[1,4096,1792]{2,1,0:T(8,128)(2,1)} %param.15), kind=kOutput, calls=%fused_computation | convolution fusion | flops 7516192768 | bytes 22544384 | tf_op jit(solution)/shard_map/dot_general | solution.py:66
  161.6 0.0 reduce-scatter.2.cloned.1.call-update
  161.6 47.4 %reduce-scatter.2.cloned.1.call-done = f32[256,1792]{1,0:T(8,128)} async-done(((f32[512,1792]{1,0:T(8,128)}), f32[256,1792]{1,0:T(8,128)}) %reduce-scatter.2.cloned.1.call-update) | async-done | bytes 1835024 | tf_op jit(solution)/shard_map/reduce_scatter | solution.py:71
  209.1 2.5 %convert_bitcast_fusion = bf16[1,256,1792]{2,1,0:T(8,128)(2,1)} fusion(f32[256,1792]{1,0:T(8,128)} %reduce-scatter.2.cloned.1.call-done), kind=kLoop, calls=%fused_computation.20 | loop fusion | flops 458752 | bytes 2752512 | tf_op jit(solution)/shard_map/broadcast_in_dim | solution.py:74
  (3 shorter events, 0.0 us)
Async XLA Ops:
  6.5 140.4 %all-gather.4.cloned.1.call-start = ((), (), s32[]{:S(2)}) async-start(), calls=%async_computation.1 | async-start | bytes 5242880 | tf_op jit(solution)/shard_map/all_gather | solution.py:67
  53.5 3.2 %copy-start = (f32[128,32,512]{2,0,1:T(8,128)}, f32[128,32,512]{2,0,1:T(8,128)S(1)}, u32[]{:S(2)}) copy-start(f32[128,32,512]{2,0,1:T(8,128)S(1)} %get-tuple-element.8) | copy-start | bytes 25165828
  67.2 141.9 %reduce-scatter.2.cloned.1.call-start = ((), (), s32[]{:S(2)}) async-start(), calls=%async_computation.2 | async-start | bytes 5505024 | tf_op jit(solution)/shard_map/reduce_scatter | solution.py:71
Sparse Core Ops, SparseCore 0:
  67.3 79.6 all-gather.3
  161.7 47.2 reduce-scatter.1
where the time goes:
time: 219 us; the launch traced here: 218 us
  waiting for transfers between devices  127 us (58%)
  matrix products  36.7 us (17%)
  blocking collectives  30 us (14%)
  between operations  13.4 us (6%)
  other arithmetic  5.9 us (3%)
  local copies, waits for them, and re-layouts  5.11 us (2%)
    all_gather x1, waiting for transfers between devices, on_device(): lax.all_gather(head_out, 'seq', axis=0, tiled=True)  79.7 us
    reduce_scatter x1, waiting for transfers between devices, on_device(): lax.psum_scatter(partial_out, 'head', scatter_dimension=0, tiled=True)  47.4 us
    all_gather x1, blocking collectives, on_device(): lat_piece = lax.all_gather(local_latent, 'seq', axis=0, tiled=True)  16.1 us
    dot_general x1, matrix products, on_device(): jnp.dot(lax.all_gather(head_out, 'seq', axis=0, tiled=True), out_weight[0...  14.6 us
    all_gather x1, blocking collectives, on_device(): lax.all_gather(local_rope, 'seq', axis=0, tiled=True)  13.9 us
    dot_general x1, matrix products, on_device(): jnp.einsum('thl,kl->thk', absorbed, lat_piece, preferred_element_type=jnp...  8.95 us
    dot_general x1, matrix products, on_device(): jnp.einsum('thl,hlv->thv', latent_out, value_up[0], preferred_element_typ...  7.97 us
    dot_general x1, matrix products, on_device(): jnp.einsum('thr,kr->thk', rope_query, lax.all_gather(local_rope, 'seq', a...  5.2 us
  transfers between devices with their start and end apart: 2, of which 2 were waited for; matrix products, arithmetic and copies ran while one was open for 0% of the time, Pallas kernels for 0%

commit v1 on v0

v1 whole, which is shorter than its diff:
```python
import jax
import jax.numpy as jnp
from jax import lax
from jax.sharding import PartitionSpec as P

NSPAN = 2

masked_fill = -1e30


def on_device(
    q_heads, cache_latent, cache_rope, span_start, prefix_len, key_up, value_up, out_weight
):
    f32, bf16 = jnp.float32, jnp.bfloat16
    queries_flat = q_heads[0]
    tokens = queries_flat.shape[0]
    head_count, nope_dim, lat_dim = key_up.shape[1:]
    value_dim = value_up.shape[3]
    head_width = queries_flat.shape[1] // head_count
    seq_count = lax.axis_size("seq")
    seq_index = lax.axis_index("seq")
    x_count = lax.axis_size("head")
    x_index = lax.axis_index("head")
    softmax_scale = head_width ** (-0.5)
    span_len = tokens * seq_count // NSPAN

    keys = lax.all_gather(
        jnp.concatenate([cache_latent[0], cache_rope[0]], axis=1), "seq", axis=0, tiled=True
    )
    latents = keys[:, :lat_dim]

    queries = queries_flat.reshape(tokens, head_count, head_width)
    absorbed = jnp.einsum(
        "thn,hnl->htl", queries[:, :, :nope_dim], key_up[0], preferred_element_type=f32
    ).astype(bf16)
    rope_query = jnp.swapaxes(queries[:, :, nope_dim:], 0, 1)
    wide = jnp.concatenate([absorbed, rope_query], axis=2)

    global_row = seq_index * tokens + jnp.arange(tokens, dtype=jnp.int32)
    one_hot = (global_row // span_len)[:, None] == jnp.arange(NSPAN, dtype=jnp.int32)[None, :]
    span_first = jnp.sum(jnp.where(one_hot, span_start[0][None, :], 0), axis=1)
    prefix_row = jnp.sum(jnp.where(one_hot, prefix_len[0][None, :], 0), axis=1)
    token_pos = span_first + global_row % span_len
    key_pos = jnp.arange(keys.shape[0], dtype=jnp.int32)
    visible = (
        (key_pos[None, :] < prefix_row[:, None])
        | (key_pos[None, :] >= span_first[:, None]) & (key_pos[None, :] <= token_pos[:, None])
    )[None]

    chunks = 4
    per = head_count // chunks
    gathered = []
    for c in range(chunks):
        sl = slice(c * per, (c + 1) * per)
        scores = jnp.einsum("htl,kl->htk", wide[sl], keys, preferred_element_type=f32)
        scores = jnp.where(visible, scores * softmax_scale, masked_fill)
        peak = jnp.max(scores, axis=2, keepdims=True)
        weights = jnp.exp(scores - peak)
        totals = jnp.sum(weights, axis=2, keepdims=True)
        summed = jnp.einsum("htk,kl->htl", weights.astype(bf16), latents, preferred_element_type=f32)
        latent_out = (summed / totals).astype(bf16)
        head_out = jnp.einsum("htl,hlv->htv", latent_out, value_up[0, sl], preferred_element_type=f32)
        head_out = jnp.swapaxes(head_out.astype(bf16), 0, 1).reshape(tokens, per * value_dim)
        gathered.append(lax.all_gather(head_out, "seq", axis=0, tiled=True))

    weight = out_weight[0]
    cut = per * value_dim * (chunks - 1)
    early = jnp.dot(
        jnp.concatenate(gathered[:-1], axis=1), weight[:cut], preferred_element_type=f32
    )
    rows = early.shape[0] // x_count

    def piece(target):
        late = lax.dynamic_slice_in_dim(gathered[-1], target * rows, rows, 0)
        return lax.dynamic_slice_in_dim(early, target * rows, rows, 0) + jnp.dot(
            late, weight[cut:], preferred_element_type=f32
        )

    arrived = []
    for shift in range(1, x_count):
        part = piece((x_index + shift) % x_count).astype(bf16)
        perm = [(i, (i + shift) % x_count) for i in range(x_count)]
        arrived.append(lax.ppermute(part, "head", perm))
    total = piece(x_index)
    for part in arrived:
        total = total + part.astype(f32)
    return total.astype(bf16)[None]


def solution(mesh):
    in_specs = (
        P("section", ("groups", "seq"), "head"),
        P("section", ("groups", "seq"), None),
        P("section", ("groups", "seq"), None),
        P("section", "groups"),
        P("section", "groups"),
        P("section", "head", None, None),
        P("section", "head", None, None),
        P("section", "head", "seq"),
    )
    out_specs = P("section", ("groups", "head"), "seq")
    return jax.shard_map(
        on_device, mesh=mesh, in_specs=in_specs, out_specs=out_specs, check_vma=False
    )
```

time: 219 us -> 209 us (0.954)
  matrix products: 36.7 us -> 53.2 us
  blocking collectives: 30 us -> 18 us
  waiting for transfers between devices: 127 us -> 115 us
  other arithmetic: 5.9 us -> 3.7 us
    reduce_scatter x1 -> x0, waiting for transfers between devices: 47.4 us -> none  [on_device(): lax.psum_scatter(partial_out, 'head', scatter_dimension=0, tiled=True)]
    ppermute x0 -> x1, waiting for transfers between devices: none -> 20.6 us  [on_device(): arrived.append(lax.ppermute(part, 'head', perm))]
    dot_general x4 -> x12, matrix products: 36.7 us -> 53.2 us  [the longest x4 14.6 us: on_device(): jnp.einsum('htl,hlv->htv', latent_out, value_up[0, sl], preferred_element...]
    all_gather x1 -> x4, waiting for transfers between devices: 79.7 us -> 94.2 us  [on_device(): gathered.append(lax.all_gather(head_out, 'seq', axis=0, tiled=True))]
    all_gather x2 -> x1, blocking collectives: 30 us -> 18 us  [on_device(): lax.all_gather(jnp.concatenate([cache_latent[0], cache_rope[0]], axis=1),...]
    broadcast_in_dim x1 -> x0, other arithmetic: 2.51 us -> none  [on_device(): return mixed_out[None]]
    unnamed x3 -> x21, local copies, waits for them, and re-layouts: 5.11 us -> 4.83 us
  transfers between devices with their start and end apart: 2 -> 5, of which waited for: 2 -> 5; matrix products, arithmetic and copies ran while one was open for 0% -> 12% of each run, Pallas kernels for 0% -> 0%
where the time goes in v1:
time: 209 us
  waiting for transfers between devices  115 us (55%)
  matrix products  53.2 us (25%)
  blocking collectives  18 us (9%)
  between operations  13.3 us (6%)
  local copies, waits for them, and re-layouts  4.86 us (2%)
  other arithmetic  3.7 us (2%)
    all_gather x4, waiting for transfers between devices, on_device(): gathered.append(lax.all_gather(head_out, 'seq', axis=0, tiled=True))  94.2 us
    ppermute x1, waiting for transfers between devices, on_device(): arrived.append(lax.ppermute(part, 'head', perm))  20.6 us
    all_gather x1, blocking collectives, on_device(): lax.all_gather(jnp.concatenate([cache_latent[0], cache_rope[0]], axis=1),...  18 us
    dot_general x4, matrix products, on_device(): jnp.einsum('htl,hlv->htv', latent_out, value_up[0, sl], preferred_element...  14.6 us
    dot_general x4, matrix products, on_device(): jnp.einsum('htl,kl->htk', wide[sl], keys, preferred_element_type=f32)  12.6 us
    dot_general x1, matrix products, on_device(): jnp.dot(jnp.concatenate(gathered[:-1], axis=1), weight[:cut], preferred_e...  12 us
    dot_general x2, matrix products, piece(): jnp.dot(late, weight[cut:], preferred_element_type=f32)  8.66 us
    dot_general x1, matrix products, on_device(): jnp.einsum('thn,hnl->htl', queries[:, :, :nope_dim], key_up[0], preferred...  5.41 us
  transfers between devices with their start and end apart: 5, of which 5 were waited for; matrix products, arithmetic and copies ran while one was open for 12% of the time, Pallas kernels for 0%

profile of v1, /device:TPU:0, one launch (start us, length us, event | category | flops | bytes accessed | tf_op | source)
XLA Modules:
  0.0 208.7 jit_solution(4805471672432958682)
XLA Ops:
  6.5 1.0 copy.33
  7.6 0.7 pad_maximum_fusion.1
  8.3 18.0 %all_gather.15 = bf16[512,576]{0,1:T(8,128)(2,1)S(1)} all-gather(bf16[128,576]{0,1:T(8,128)(2,1)S(1)} %pad_maximum_fusion.1), channel_id=1, replica_groups=mesh['groups'=2,'seq'=4,'head'=2,'section'=2] {'seq'}, dimensions={0}, use_global_device_ids=true | all-gather | bytes 737280 | tf_op jit(solution)/shard_map/all_gather | solution.py:27
  26.3 1.9 copy.30
  28.2 5.4 %fusion.22 = bf16[32,128,512]{2,1,0:T(8,128)(2,1)} fusion(bf16[1,32,128,512]{3,2,1,0:T(8,128)(2,1)} %param.13, bf16[128,32,192]{0,2,1:T(8,128)(2,1)S(1)} %bitcast.90), kind=kOutput, calls=%fused_computation.19 | convolution fusion | flops 538968064 | bytes 9437184 | tf_op jit(solution)/shard_map/thn,hnl->htl/dot_general | solution.py:33
  33.7 0.5 copy.59
  34.2 3.7 %fusion.112 = f32[8,128,512]{2,1,0:T(8,128)} fusion(bf16[512,576]{0,1:T(8,128)(2,1)S(1)} %all_gather.15, bf16[32,128,64]{2,1,0:T(8,128)(2,1)S(1)} %bitcast.85, bf16[32,128,512]{2,1,0:T(8,128)(2,1)} %fusion.22), kind=kOutput, calls=%fused_computation.90 | convolution fusion | flops 613416960 | bytes 7405568 | tf_op jit(solution)/shard_map/htl,kl->htk/dot_general | solution.py:55
  37.9 2.3 %fusion.108 = f32[8,128,512]{2,1,0:T(8,128)} fusion(bf16[512,576]{0,1:T(8,128)(2,1)S(1)} %all_gather.15, bf16[32,128,64]{2,1,0:T(8,128)(2,1)S(1)} %bitcast.86, bf16[32,128,512]{2,1,0:T(8,128)(2,1)S(1)} %copy-done), kind=kOutput, calls=%fused_computation.86 | convolution fusion | flops 613416960 | bytes 7405568 | tf_op jit(solution)/shard_map/htl,kl->htk/dot_general | solution.py:55
  40.3 0.1 select_reduce_fusion.1
  40.4 0.2 fusion.116
  40.5 3.2 %fusion.31 = (f32[8,128]{1,0:T(8,128)S(1)}, f32[8,128]{1,0:T(8,128)S(1)}, f32[8,128,512]{2,1,0:T(8,128)S(1)}) fusion(pred[128,512]{1,0:T(8,128)(4,1)S(1)} %fusion.116, f32[8,128,512]{2,1,0:T(8,128)} %fusion.112, bf16[512,576]{0,1:T(8,128)(2,1)S(1)} %all_gather.15, bf16[32,128,64]{2,1,0:T(8,128)(2,1)S(1)} %bitcast.87, bf16[32,128,512]{2,1,0:T(8,128)(2,1)} %fusion.22), kind=kOutput, calls=%fused_computation.36 | convolution fusion | flops 616560640 | bytes 9576448 | tf_op jit(solution)/shard_map/htl,kl->htk/dot_general | solution.py:55
  43.8 0.5 copy-done.2
  44.3 0.9 copy-done.4
  45.2 3.3 %fusion.43 = (f32[8,128]{1,0:T(8,128)S(1)}, f32[8,128]{1,0:T(8,128)S(1)}, f32[8,128]{1,0:T(8,128)S(1)}, f32[8,128]{1,0:T(8,128)S(1)}, f32[8,128,512]{2,1,0:T(8,128)}) fusion(f32[8,128,512]{2,1,0:T(8,128)S(1)} %get-tuple-element.15, f32[8,128]{1,0:T(8,128)S(1)} %get-tuple-element.9, pred[128,512]{1,0:T(8,128)(4,1)S(1)} %fusion.116, ...), kind=kOutput, calls=%fused_computation.45 | convolution fusion | flops 620752896 | bytes 13787136 | tf_op jit(solution)/shard_map/htl,kl->htk/dot_general | solution.py:55
  48.5 3.9 %fusion.52 = bf16[8,128,128]{1,2,0:T(8,128)(2,1)} fusion(f32[8,128,512]{2,1,0:T(8,128)} %fusion.112, bf16[1,32,512,128]{3,2,1,0:T(8,128)(2,1)} %param.14, f32[8,128]{1,0:T(8,128)S(1)} %get-tuple-element.8, f32[8,128]{1,0:T(8,128)S(1)} %get-tuple-element.10, pred[128,512]{1,0:T(8,128)(4,1)S(1)} %fusion.116, bf16[512,576]{0,1:T(8,128)(2,1)S(1)} %all_gather.15), kind=kOutput, calls=%fused_computation.54 | convolution fusion | flops 674365440 | bytes 4005888 | tf_op jit(solution)/shard_map/htl,hlv->htv/dot_general | solution.py:62
  52.5 0.0 all-gather.5.cloned.1.call-update
  52.5 0.0 all-gather.7.cloned.1.call-start
  52.6 2.7 %fusion.39 = (f32[8,128]{1,0:T(8,128)S(1)}, f32[8,128]{1,0:T(8,128)S(1)}) fusion(f32[8,128,512]{2,1,0:T(8,128)} %get-tuple-element.16, f32[8,128]{1,0:T(8,128)S(1)} %get-tuple-element.6, pred[128,512]{1,0:T(8,128)(4,1)S(1)} %fusion.116, f32[8,128]{1,0:T(8,128)S(1)} %get-tuple-element.7, f32[8,128,512]{2,1,0:T(8,128)S(1)} %copy-done.3), kind=kLoop, calls=%fused_computation.41 | loop fusion | flops 4192256 | bytes 4276224 | tf_op jit(solution)/shard_map/reduce_sum | solution.py:59
  55.2 3.8 %fusion.51 = bf16[8,128,128]{1,2,0:T(8,128)(2,1)} fusion(f32[8,128,512]{2,1,0:T(8,128)} %get-tuple-element.16, bf16[1,32,512,128]{3,2,1,0:T(8,128)(2,1)} %param.14, f32[8,128]{1,0:T(8,128)S(1)} %get-tuple-element.11, f32[8,128]{1,0:T(8,128)S(1)} %get-tuple-element.6, pred[128,512]{1,0:T(8,128)(4,1)S(1)} %fusion.116, bf16[512,576]{0,1:T(8,128)(2,1)S(1)} %all_gather.15), kind=kOutput, calls=%fused_computation.53 | convolution fusion | flops 674365440 | bytes 4005888 | tf_op jit(solution)/shard_map/htl,hlv->htv/dot_general | solution.py:62
  59.0 0.0 all-gather.9.cloned.1.call-start
  59.1 3.1 %fusion.50 = bf16[8,128,128]{1,2,0:T(8,128)(2,1)} fusion(f32[8,128,512]{2,1,0:T(8,128)S(1)} %copy-done.3, bf16[1,32,512,128]{3,2,1,0:T(8,128)(2,1)} %param.14, f32[8,128]{1,0:T(8,128)S(1)} %get-tuple-element.12, f32[8,128]{1,0:T(8,128)S(1)} %get-tuple-element.7, pred[128,512]{1,0:T(8,128)(4,1)S(1)} %fusion.116, bf16[512,576]{0,1:T(8,128)(2,1)S(1)} %all_gather.15), kind=kOutput, calls=%fused_computation.52 | convolution fusion | flops 674365440 | bytes 4005888 | tf_op jit(solution)/shard_map/htl,hlv->htv/dot_general | solution.py:62
  62.2 0.2 all-gather.11.cloned.1.call-start
  62.5 3.8 %fusion.49 = bf16[8,128,128]{1,2,0:T(8,128)(2,1)} fusion(f32[8,128,512]{2,1,0:T(8,128)} %copy-done.5, bf16[1,32,512,128]{3,2,1,0:T(8,128)(2,1)} %param.14, f32[8,128]{1,0:T(8,128)S(1)} %get-tuple-element.5, f32[8,128]{1,0:T(8,128)S(1)} %get-tuple-element.9, pred[128,512]{1,0:T(8,128)(4,1)S(1)} %fusion.116, bf16[512,576]{0,1:T(8,128)(2,1)S(1)} %all_gather.15), kind=kOutput, calls=%fused_computation.51 | convolution fusion | flops 674365440 | bytes 4005888 | tf_op jit(solution)/shard_map/htl,hlv->htv/dot_general | solution.py:62
  66.3 16.0 %all-gather.5.cloned.1.call-done = bf16[512,1024]{0,1:T(8,128)(2,1)} async-done(((bf16[128,1024]{0,1:T(8,128)(2,1)}), bf16[512,1024]{0,1:T(8,128)(2,1)}) %all-gather.5.cloned.1.call-update) | async-done | bytes 1048592 | tf_op jit(solution)/shard_map/all_gather | solution.py:64
  82.3 30.1 %all-gather.7.cloned.1.call-done = bf16[512,1024]{0,1:T(8,128)(2,1)} async-done(((bf16[128,1024]{0,1:T(8,128)(2,1)}), bf16[512,1024]{0,1:T(8,128)(2,1)}) %all-gather.7.cloned.1.call-update) | async-done | bytes 1048592 | tf_op jit(solution)/shard_map/all_gather | solution.py:64
  112.4 30.1 %all-gather.9.cloned.1.call-done = bf16[512,1024]{0,1:T(8,128)(2,1)} async-done(((bf16[128,1024]{0,1:T(8,128)(2,1)}), bf16[512,1024]{0,1:T(8,128)(2,1)}) %all-gather.9.cloned.1.call-update) | async-done | bytes 1048592 | tf_op jit(solution)/shard_map/all_gather | solution.py:64
  142.5 12.0 %fusion = f32[512,1792]{1,0:T(8,128)} fusion(bf16[1,4096,1792]{2,1,0:T(8,128)(2,1)} %param.15, bf16[512,1024]{0,1:T(8,128)(2,1)} %all-gather.9.cloned.1.call-done, bf16[512,1024]{0,1:T(8,128)(2,1)} %all-gather.7.cloned.1.call-done, bf16[512,1024]{0,1:T(8,128)(2,1)} %all-gather.5.cloned.1.call-done), kind=kOutput, calls=%fused_computation | convolution fusion | flops 5646581760 | bytes 17825792 | tf_op jit(solution)/shard_map/dot_general | solution.py:68
  154.4 18.0 %all-gather.11.cloned.1.call-done = bf16[512,1024]{0,1:T(8,128)(2,1)} async-done(((bf16[128,1024]{0,1:T(8,128)(2,1)}), bf16[512,1024]{0,1:T(8,128)(2,1)}) %all-gather.11.cloned.1.call-update) | async-done | bytes 1048592 | tf_op jit(solution)/shard_map/all_gather | solution.py:64
  172.4 4.0 %fusion.25 = bf16[256,1792]{1,0:T(8,128)(2,1)S(1)} fusion(bf16[1,4096,1792]{2,1,0:T(8,128)(2,1)} %param.15, f32[512,1792]{1,0:T(8,128)} %fusion, s32[]{:T(128)S(6)} %select_n.64, bf16[512,1024]{0,1:T(8,128)(2,1)} %all-gather.11.cloned.1.call-done), kind=kOutput, calls=%fused_computation.20 | convolution fusion | flops 940441600 | bytes 6947840 | tf_op jit(solution)/shard_map/dot_general | solution.py:75
  176.4 0.5 collective-permute-start
  176.9 20.6 %collective-permute-done = bf16[256,1792]{1,0:T(8,128)(2,1)S(1)} collective-permute-done((bf16[256,1792]{1,0:T(8,128)(2,1)S(1)}, bf16[256,1792]{1,0:T(8,128)(2,1)S(1)}, u32[]{:S(2)}, u32[]{:S(2)}) %collective-permute-start) | collective-permute-done | bytes 917536 | tf_op jit(solution)/shard_map/ppermute | solution.py:83
  197.5 4.7 %fusion.34 = bf16[1,256,1792]{2,1,0:T(8,128)(2,1)} fusion(bf16[256,1792]{1,0:T(8,128)(2,1)S(1)} %collective-permute-done, bf16[1,4096,1792]{2,1,0:T(8,128)(2,1)} %param.15, f32[512,1792]{1,0:T(8,128)} %fusion, s32[]{:T(128)S(6)} %select_n.61, bf16[512,1024]{0,1:T(8,128)(2,1)S(1)} %copy-done.8), kind=kOutput, calls=%fused_computation.38 | convolution fusion | flops 941359104 | bytes 7865344 | tf_op jit(solution)/shard_map/dot_general | solution.py:75
  (23 shorter events, 0.1 us)
Async XLA Ops:
  6.5 75.7 %all-gather.5.cloned.1.call-start = ((), (), s32[]{:S(2)}) async-start(), calls=%async_computation | async-start | bytes 1310720 | tf_op jit(solution)/shard_map/all_gather | solution.py:64
  34.1 3.8 %copy-start = (bf16[32,128,512]{2,1,0:T(8,128)(2,1)S(1)}, bf16[32,128,512]{2,1,0:T(8,128)(2,1)}, u32[]{:S(2)}) copy-start(bf16[32,128,512]{2,1,0:T(8,128)(2,1)} %fusion.22) | copy-start | bytes 12582916
  37.9 2.3 %copy-start.6 = (s32[1,2]{1,0:T(1,128)S(1)}, s32[1,2]{1,0:T(1,128)}, u32[]{:S(2)}) copy-start(s32[1,2]{1,0:T(1,128)} %param.12) | copy-start | bytes 28
  37.9 2.3 %copy-start.7 = (s32[1,2]{1,0:T(1,128)S(1)}, s32[1,2]{1,0:T(1,128)}, u32[]{:S(2)}) copy-start(s32[1,2]{1,0:T(1,128)} %param.11) | copy-start | bytes 28
  40.5 3.3 %copy-start.1 = (bf16[32,128,512]{2,1,0:T(8,128)(2,1)S(1)}, bf16[32,128,512]{2,1,0:T(8,128)(2,1)}, u32[]{:S(2)}) copy-start(bf16[32,128,512]{2,1,0:T(8,128)(2,1)} %fusion.22) | copy-start | bytes 12582916
  40.5 3.8 %copy-start.2 = (f32[8,128,512]{2,1,0:T(8,128)S(1)}, f32[8,128,512]{2,1,0:T(8,128)}, u32[]{:S(2)}) copy-start(f32[8,128,512]{2,1,0:T(8,128)} %fusion.108) | copy-start | bytes 6291460
  40.5 4.7 %copy-start.4 = (f32[8,128,512]{2,1,0:T(8,128)S(1)}, f32[8,128,512]{2,1,0:T(8,128)}, u32[]{:S(2)}) copy-start(f32[8,128,512]{2,1,0:T(8,128)} %fusion.112) | copy-start | bytes 6291460
  43.8 4.7 %copy-start.5 = (f32[8,128,512]{2,1,0:T(8,128)}, f32[8,128,512]{2,1,0:T(8,128)S(1)}, u32[]{:S(2)}) copy-start(f32[8,128,512]{2,1,0:T(8,128)S(1)} %get-tuple-element.15) | copy-start | bytes 6291460
  48.5 4.0 %copy-start.3 = (f32[8,128,512]{2,1,0:T(8,128)S(1)}, f32[8,128,512]{2,1,0:T(8,128)}, u32[]{:S(2)}) copy-start(f32[8,128,512]{2,1,0:T(8,128)} %fusion.108) | copy-start | bytes 6291460
  52.5 59.9 %all-gather.7.cloned.1.call-start = ((), (), s32[]{:S(2)}) async-start(), calls=%async_computation.1 | async-start | bytes 1310720 | tf_op jit(solution)/shard_map/all_gather | solution.py:64
  59.0 83.4 %all-gather.9.cloned.1.call-start = ((), (), s32[]{:S(2)}) async-start(), calls=%async_computation.2 | async-start | bytes 1310720 | tf_op jit(solution)/shard_map/all_gather | solution.py:64
  62.2 110.2 %all-gather.11.cloned.1.call-start = ((), (), s32[]{:S(2)}) async-start(), calls=%async_computation.3 | async-start | bytes 1310720 | tf_op jit(solution)/shard_map/all_gather | solution.py:64
  172.4 25.1 %copy-start.8 = (bf16[512,1024]{0,1:T(8,128)(2,1)S(1)}, bf16[512,1024]{0,1:T(8,128)(2,1)}, u32[]{:S(2)}) copy-start(bf16[512,1024]{0,1:T(8,128)(2,1)} %all-gather.11.cloned.1.call-done) | copy-start | bytes 3145732
  176.4 21.1 %collective-permute-start = (bf16[256,1792]{1,0:T(8,128)(2,1)S(1)}, bf16[256,1792]{1,0:T(8,128)(2,1)S(1)}, u32[]{:S(2)}, u32[]{:S(2)}) collective-permute-start(bf16[256,1792]{1,0:T(8,128)(2,1)S(1)} %fusion.25), channel_id=1, source_target_pairs={{0,2},{2,0},{1,3},{3,1},{4,6},{6,4},{5,7},{7,5},{8,10},{10,8},{9,1... | collective-permute-start | bytes 2752520 | tf_op jit(solution)/shard_map/ppermute | solution.py:83
Sparse Core Ops, SparseCore 0:
  52.6 29.5 all-gather.4
  83.8 28.4 all-gather.6
  113.9 28.4 all-gather.8
  143.9 28.4 all-gather.10

commit v2 on v0

v2 whole, which is shorter than its diff:
```python
import functools
import math

import jax
import jax.numpy as jnp
from jax import lax
from jax.experimental import pallas as pl
from jax.experimental.pallas import tpu as pltpu
from jax.sharding import PartitionSpec as P

NSPAN = 2
SPLIT = 2
masked_fill = -1e30
f32, bf16 = jnp.float32, jnp.bfloat16


def kernel(
    n, xn, kv_ref, start_ref, prefix_ref, q_hbm, ku_hbm, vu_hbm, w_hbm, out_ref,
    keys, q, ku, vu, w, wide, bias, full, acc, xs, xr,
    lsem, kv_ssem, kv_rsem, z_ssem, z_rsem, x_ssem, x_rsem,
):
    me = lax.axis_index("seq")
    xi = lax.axis_index("head")
    tokens = kv_ref.shape[0]
    heads, nope, lat = ku.shape
    vdim = vu.shape[2]
    pair = 2 * q.shape[1] // heads
    rope = pair // 2 - nope
    units, hgs, ts, hw = full.shape
    hg_heads = hw // vdim
    upx, ntiles, _, nt = acc.shape
    ctx = n * tokens
    scale = math.log2(math.e) * (pair // 2) ** (-0.5)

    loads = [
        pltpu.make_async_copy(a, b, lsem.at[i])
        for i, (a, b) in enumerate(((q_hbm, q), (ku_hbm, ku), (vu_hbm, vu), (w_hbm, w)))
    ]
    for load in loads:
        load.start()

    barrier = pltpu.get_barrier_semaphore()
    has_left, has_right = me > 0, me < n - 1

    def greet(**where):
        pl.semaphore_signal(
            barrier, inc=1, device_id=where, device_id_type=pl.DeviceIdType.MESH
        )

    @pl.when(has_left)
    def _():
        greet(seq=me - 1)

    @pl.when(has_right)
    def _():
        greet(seq=me + 1)

    for s in range(1, xn):
        greet(head=lax.rem(xi + s, xn))

    for part in range(SPLIT):
        keys[me * SPLIT + part] = kv_ref[part * ts : (part + 1) * ts, :]

    met = xn - 1 + jnp.minimum(me, 1) + jnp.minimum(n - 1 - me, 1)
    pl.semaphore_wait(barrier, met)

    def kv_copy(i, way):
        return pltpu.make_async_remote_copy(
            src_ref=keys.at[i],
            dst_ref=keys.at[i],
            send_sem=kv_ssem.at[way, i],
            recv_sem=kv_rsem.at[i],
            device_id={"seq": me - 1 + 2 * way},
            device_id_type=pl.DeviceIdType.MESH,
        )

    def z_copy(unit, hg, way):
        return pltpu.make_async_remote_copy(
            src_ref=full.at[unit, hg],
            dst_ref=full.at[unit, hg],
            send_sem=z_ssem.at[way, unit, hg],
            recv_sem=z_rsem.at[unit, hg],
            device_id={"seq": me - 1 + 2 * way},
            device_id_type=pl.DeviceIdType.MESH,
        )

    def send_own(make):
        @pl.when(has_left)
        def _():
            make(0).start()

        @pl.when(has_right)
        def _():
            make(1).start()

    def take(make, d, wait=True):
        @pl.when(me + d < n)
        def _():
            make(me + d, 1).wait_recv()

            @pl.when(has_left)
            def _():
                make(me + d, 0).start()

        @pl.when(me - d >= 0)
        def _():
            make(me - d, 0).wait_recv()

            @pl.when(has_right)
            def _():
                make(me - d, 1).start()

    for part in range(SPLIT):
        send_own(lambda way, part=part: kv_copy(me * SPLIT + part, way))

    def absorb(i, _):
        block = q[:, pl.ds(pl.multiple_of(i * pair, pair), pair)]
        lead = jnp.zeros((rope, lat), bf16)
        tail = lead
        first = jnp.dot(block[:, :nope], ku[2 * i], preferred_element_type=f32)
        second = jnp.dot(
            block[:, nope:],
            jnp.concatenate([lead, ku[2 * i + 1], tail], axis=0),
            preferred_element_type=f32,
        )
        lane = lax.broadcasted_iota(jnp.int32, (tokens, 2 * rope), 1)
        zero = jnp.zeros((tokens, 2 * rope), bf16)
        wide[2 * i, :, :lat] = first.astype(bf16)
        wide[2 * i + 1, :, :lat] = second.astype(bf16)
        wide[2 * i, :, lat:] = jnp.where(lane < rope, block[:, nope : nope + 2 * rope], zero)
        wide[2 * i + 1, :, lat:] = jnp.where(lane >= rope, block[:, pair - 2 * rope :], zero)
        return 0

    loads[0].wait()
    loads[1].wait()

    span_len = ctx // NSPAN
    span = me * tokens // span_len
    first_pos = start_ref[0, span]
    prefix = prefix_ref[0, span]
    row_pos = first_pos + me * tokens % span_len + lax.broadcasted_iota(jnp.int32, (tokens, ctx), 0)
    key_pos = lax.broadcasted_iota(jnp.int32, (tokens, ctx), 1)
    visible = (key_pos < prefix) | ((key_pos >= first_pos) & (key_pos <= row_pos))
    bias[...] = jnp.where(visible, 0.0, masked_fill)

    half = heads // 4
    lax.fori_loop(0, half, absorb, 0)
    for d in range(1, n):
        for part in range(SPLIT):
            take(lambda src, way, part=part: kv_copy(src * SPLIT + part, way), d)
        if d == 1:
            lax.fori_loop(half, heads // 2, absorb, 0)
    loads[2].wait()

    def attend(m, _):
        tb, hg = m // hgs, lax.rem(m, hgs)
        rows = pl.ds(pl.multiple_of(tb * ts, ts), ts)
        unit = me * SPLIT + tb
        all_keys = keys[...].reshape(ctx, keys.shape[2])
        hide = bias[rows, :]
        for p in range(hg_heads // 2):
            h = hg * hg_heads + 2 * p
            wq = wide[pl.ds(h, 2), rows, :].reshape(2 * ts, wide.shape[2])
            scores = lax.dot_general(
                wq, all_keys, (((1,), (1,)), ((), ())), preferred_element_type=f32
            )
            scores = scores * scale + jnp.concatenate([hide, hide], axis=0)
            peak = jnp.max(scores, axis=1, keepdims=True)
            weights = jnp.exp2(scores - peak)
            total = jnp.sum(weights, axis=1, keepdims=True)
            mixed = jnp.dot(weights.astype(bf16), all_keys[:, :lat], preferred_element_type=f32)
            mixed = (mixed / total).astype(bf16)
            for k in range(2):
                value = jnp.dot(
                    mixed[k * ts : (k + 1) * ts], vu[h + k], preferred_element_type=f32
                )
                lo = (2 * p + k) * vdim
                full[unit, hg, :, lo : lo + vdim] = value.astype(bf16)
        send_own(lambda way: z_copy(unit, hg, way))
        return 0

    lax.fori_loop(0, SPLIT * hgs, attend, 0)

    def x_copy(unit, t):
        return pltpu.make_async_remote_copy(
            src_ref=xs.at[unit, t],
            dst_ref=xr.at[xi, lax.rem(unit, upx), t],
            send_sem=x_ssem.at[unit, t],
            recv_sem=x_rsem.at[xi, lax.rem(unit, upx), t],
            device_id={"head": unit // upx},
            device_id_type=pl.DeviceIdType.MESH,
        )

    def project(unit):
        mine = unit // upx == xi

        def tile(t, _):
            total = jnp.zeros((ts, nt), f32)
            for hg in range(hgs):
                if ntiles == 1:
                    part = w[hg * hw : (hg + 1) * hw, :]
                else:
                    part = w[hg * hw : (hg + 1) * hw, pl.ds(pl.multiple_of(t * nt, nt), nt)]
                total += jnp.dot(full[unit, hg], part, preferred_element_type=f32)

            @pl.when(mine)
            def _():
                acc[lax.rem(unit, upx), t] = total

            @pl.when(jnp.logical_not(mine))
            def _():
                xs[unit, t] = total.astype(bf16)
                x_copy(unit, t).start()

            return 0

        lax.fori_loop(0, ntiles, tile, 0)

    loads[3].wait()

    for tb in range(SPLIT):
        project(me * SPLIT + tb)

    def gather(i, _):
        d, tb = 1 + i // SPLIT, lax.rem(i, SPLIT)
        for hg in range(hgs):
            take(lambda src, way, hg=hg: z_copy(src * SPLIT + tb, hg, way), d)

        @pl.when(me + d < n)
        def _():
            project((me + d) * SPLIT + tb)

        @pl.when(me - d >= 0)
        def _():
            project((me - d) * SPLIT + tb)

        return 0

    lax.fori_loop(0, (n - 1) * SPLIT, gather, 0)

    def sent(i, _):
        unit = i
        left = has_left & (unit >= me * SPLIT)
        right = has_right & (unit < (me + 1) * SPLIT)
        for way, did in ((0, left), (1, right)):

            @pl.when(did)
            def _():
                kv_copy(unit, way).wait_send()
                for hg in range(hgs):
                    z_copy(unit, hg, way).wait_send()

        return 0

    lax.fori_loop(0, units, sent, 0)

    for lu in range(upx):
        for t in range(ntiles):
            total = acc[lu, t]
            for s in range(1, xn):
                peer = lax.rem(xi + s, xn)
                pltpu.make_async_remote_copy(
                    src_ref=xs.at[0, t],
                    dst_ref=xr.at[peer, lu, t],
                    send_sem=x_ssem.at[0, t],
                    recv_sem=x_rsem.at[peer, lu, t],
                    device_id={"head": peer},
                    device_id_type=pl.DeviceIdType.MESH,
                ).wait_recv()
                total = total + xr[peer, lu, t].astype(f32)
            out_ref[lu * ts : (lu + 1) * ts, t * nt : (t + 1) * nt] = total.astype(bf16)

    def x_sent(i, _):
        @pl.when(i // upx != xi)
        def _():
            for t in range(ntiles):
                x_copy(i, t).wait_send()

        return 0

    lax.fori_loop(0, units, x_sent, 0)


def on_device(
    n, xn, q_heads, cache_latent, cache_rope, span_start, prefix_len, key_up, value_up, out_weight
):
    heads, nope, lat = key_up.shape[1:]
    vdim = value_up.shape[3]
    tokens = q_heads.shape[1]
    rope = cache_rope.shape[2]
    rows_all, width = out_weight.shape[1:]
    keys = jnp.concatenate([cache_latent[0], cache_rope[0], cache_rope[0]], axis=1)
    kw = lat + 2 * rope
    ts = tokens // SPLIT
    units = n * SPLIT
    upx = units // xn
    hg_heads = math.gcd(8, heads)
    hgs = heads // hg_heads
    nt = 256 if width % 256 == 0 else width
    ntiles = width // nt
    ctx = n * tokens
    vmem, smem = pltpu.VMEM, pltpu.SMEM
    hbm = pl.BlockSpec(memory_space=pl.ANY)
    out = pl.pallas_call(
        functools.partial(kernel, n, xn),
        out_shape=jax.ShapeDtypeStruct((upx * ts, width), bf16),
        in_specs=[
            pl.BlockSpec(memory_space=vmem),
            pl.BlockSpec(memory_space=smem),
            pl.BlockSpec(memory_space=smem),
            hbm,
            hbm,
            hbm,
            hbm,
        ],
        out_specs=pl.BlockSpec(memory_space=vmem),
        scratch_shapes=[
            vmem((units, ts, kw), bf16),
            vmem(q_heads.shape[1:], bf16),
            vmem(key_up.shape[1:], bf16),
            vmem(value_up.shape[1:], bf16),
            vmem((rows_all, width), bf16),
            vmem((heads, tokens, kw), bf16),
            vmem((tokens, ctx), f32),
            vmem((units, hgs, ts, hg_heads * vdim), bf16),
            vmem((upx, ntiles, ts, nt), f32),
            vmem((units, ntiles, ts, nt), bf16),
            vmem((xn, upx, ntiles, ts, nt), bf16),
            pltpu.SemaphoreType.DMA((4,)),
            pltpu.SemaphoreType.DMA((2, units)),
            pltpu.SemaphoreType.DMA((units,)),
            pltpu.SemaphoreType.DMA((2, units, hgs)),
            pltpu.SemaphoreType.DMA((units, hgs)),
            pltpu.SemaphoreType.DMA((units, ntiles)),
            pltpu.SemaphoreType.DMA((xn, upx, ntiles)),
        ],
        compiler_params=pltpu.CompilerParams(
            collective_id=0, has_side_effects=True, vmem_limit_bytes=56 * 1024 * 1024
        ),
        cost_estimate=pl.CostEstimate(
            flops=2 * ctx * rows_all * width + 4 * tokens * heads * ctx * kw,
            bytes_accessed=2 * rows_all * width,
            transcendentals=tokens * heads * ctx,
        ),
    )(keys, span_start, prefix_len, q_heads[0], key_up[0], value_up[0], out_weight[0])
    return out[None]


def solution(mesh):
    in_specs = (
        P("section", ("groups", "seq"), "head"),
        P("section", ("groups", "seq"), None),
        P("section", ("groups", "seq"), None),
        P("section", "groups"),
        P("section", "groups"),
        P("section", "head", None, None),
        P("section", "head", None, None),
        P("section", "head", "seq"),
    )
    out_specs = P("section", ("groups", "head"), "seq")
    return jax.shard_map(
        functools.partial(on_device, mesh.shape["seq"], mesh.shape["head"]),
        mesh=mesh,
        in_specs=in_specs,
        out_specs=out_specs,
        check_vma=False,
    )
```

time: 219 us -> 100 us (0.46)
  waiting for transfers between devices: 127 us -> 0 us
  Pallas kernels: 0 us -> 95.1 us
  matrix products: 36.7 us -> 0 us
  blocking collectives: 30 us -> 0 us
  between operations: 13.4 us -> 0.01 us
  other arithmetic: 5.9 us -> 1.66 us
    pallas_call x0 -> x1, Pallas kernels: none -> 95.1 us  [on_device(): pl.pallas_call(functools.partial(kernel, n, xn), out_shape=jax.ShapeDtype...]
    all_gather x1 -> x0, waiting for transfers between devices: 79.7 us -> none  [on_device(): lax.all_gather(head_out, 'seq', axis=0, tiled=True)]
    reduce_scatter x1 -> x0, waiting for transfers between devices: 47.4 us -> none  [on_device(): lax.psum_scatter(partial_out, 'head', scatter_dimension=0, tiled=True)]
    dot_general x4 -> x0, matrix products: 36.7 us -> none  [the longest x1 14.6 us: on_device(): jnp.dot(lax.all_gather(head_out, 'seq', axis=0, tiled=True), out_weight[0...]
    all_gather x2 -> x0, blocking collectives: 30 us -> none  [the longest x1 16.1 us: on_device(): lat_piece = lax.all_gather(local_latent, 'seq', axis=0, tiled=True)]
    reduce_sum x2 -> x0, other arithmetic: 3.2 us -> none  [the longest x1 2.44 us: on_device(): totals = jnp.sum(weights, axis=2)]
    broadcast_in_dim x1 -> x0, other arithmetic: 2.51 us -> none  [on_device(): return mixed_out[None]]
    unnamed x3 -> x2, local copies, waits for them, and re-layouts: 5.11 us -> 2.98 us
  transfers between devices with their start and end apart: 2 -> 0, of which waited for: 2 -> 0; matrix products, arithmetic and copies ran while one was open for 0% -> 0% of each run, Pallas kernels for 0% -> 0%
where the time goes in v2:
time: 100 us; the launch traced here: 99.7 us
  Pallas kernels  95.1 us (95%)
  local copies, waits for them, and re-layouts  2.98 us (3%)
  other arithmetic  1.66 us (2%)
    pallas_call x1, Pallas kernels, on_device(): pl.pallas_call(functools.partial(kernel, n, xn), out_shape=jax.ShapeDtype...  95.1 us
    unnamed x2, local copies, waits for them, and re-layouts  2.98 us

profile of v2, /device:TPU:0, one launch (start us, length us, event | category | flops | bytes accessed | tf_op | source)
XLA Modules:
  0.0 99.7 jit_solution(1397704082082112203)
XLA Ops:
  0.0 0.8 copy.9
  0.8 1.7 %pad_maximum_fusion.kv_ref = bf16[128,640]{1,0:T(8,128)(2,1)} fusion(bf16[128,64]{1,0:T(8,128)(2,1)S(1)} %bitcast.8, bf16[128,512]{1,0:T(8,128)(2,1)} %bitcast.9), kind=kLoop, calls=%fused_computation | loop fusion | flops 491520 | bytes 311296 | tf_op jit(solution)/shard_map/concatenate | solution.py:292
  2.5 95.1 %shard_map.82 = bf16[256,1792]{1,0:T(8,128)(2,1)} custom-call(bf16[128,640]{1,0:T(8,128)(2,1)} %pad_maximum_fusion.kv_ref, s32[1,2]{1,0:T(1,128)} %start_ref.1, s32[1,2]{1,0:T(1,128)} %prefix_ref.1, bf16[128,6144]{1,0:T(8,128)(2,1)} %bitcast.13, bf16[32,128,512]{2,1,0:T(8,128)(2,1)} %bitcast.11, bf16[32,512,128]{2,1,0:T(8,128)(2,1)} %bitcast.12, ...), custom_call_target="tpu_custom_call" | custom-call | flops 12884901888 | bytes 14680064 | tf_op jit(solution)/shard_map/pallas_call | solution.py:304
  97.6 2.2 %copy.11 = bf16[1,256,1792]{2,1,0:T(8,128)(2,1)} copy(bf16[1,256,1792]{2,1,0:T(8,128)(2,1)} %bitcast.7) | data formatting | bytes 1835008

commit v3 on v2

--- a/solution.py
+++ b/solution.py
@@ -9,25 +9,26 @@
 from jax.sharding import PartitionSpec as P
 
 NSPAN = 2
-SPLIT = 2
+SPLIT = 4
 masked_fill = -1e30
 f32, bf16 = jnp.float32, jnp.bfloat16
 
 
 def kernel(
-    n, xn, kv_ref, start_ref, prefix_ref, q_hbm, ku_hbm, vu_hbm, w_hbm, out_ref,
+    n, xn, lat_ref, rope_ref, start_ref, prefix_ref, q_hbm, ku_hbm, vu_hbm, w_hbm, out_ref,
     keys, q, ku, vu, w, wide, bias, full, acc, xs, xr,
-    lsem, kv_ssem, kv_rsem, z_ssem, z_rsem, x_ssem, x_rsem,
+    lsem, kv_ssem, kv_rsem, kx_ssem, z_ssem, z_rsem, x_ssem, x_rsem,
 ):
     me = lax.axis_index("seq")
     xi = lax.axis_index("head")
-    tokens = kv_ref.shape[0]
+    tokens = lat_ref.shape[0]
     heads, nope, lat = ku.shape
     vdim = vu.shape[2]
     pair = 2 * q.shape[1] // heads
     rope = pair // 2 - nope
     units, hgs, ts, hw = full.shape
     hg_heads = hw // vdim
+    batch = min(4, hg_heads)
     upx, ntiles, _, nt = acc.shape
     ctx = n * tokens
     scale = math.log2(math.e) * (pair // 2) ** (-0.5)
@@ -58,8 +59,12 @@
     for s in range(1, xn):
         greet(head=lax.rem(xi + s, xn))
 
-    for part in range(SPLIT):
-        keys[me * SPLIT + part] = kv_ref[part * ts : (part + 1) * ts, :]
+    kr = tokens // xn
+    twice = jnp.concatenate([rope_ref[...], rope_ref[...]], axis=1)
+    for part in range(xn):
+        rows = slice(part * kr, (part + 1) * kr)
+        keys[me * xn + part, :, :lat] = lat_ref[rows, :]
+        keys[me * xn + part, :, lat:] = twice[rows]
 
     met = xn - 1 + jnp.minimum(me, 1) + jnp.minimum(n - 1 - me, 1)
     pl.semaphore_wait(barrier, met)
@@ -74,6 +79,16 @@
             device_id_type=pl.DeviceIdType.MESH,
         )
 
+    def kx_copy(i, s):
+        return pltpu.make_async_remote_copy(
+            src_ref=keys.at[i],
+            dst_ref=keys.at[i],
+            send_sem=kx_ssem.at[s, i],
+            recv_sem=kv_rsem.at[i],
+            device_id={"head": lax.rem(xi + s, xn)},
+            device_id_type=pl.DeviceIdType.MESH,
+        )
+
     def z_copy(unit, hg, way):
         return pltpu.make_async_remote_copy(
             src_ref=full.at[unit, hg],
@@ -93,7 +108,7 @@
         def _():
             make(1).start()
 
-    def take(make, d, wait=True):
+    def take(make, d, after=None):
         @pl.when(me + d < n)
         def _():
             make(me + d, 1).wait_recv()
@@ -102,6 +117,9 @@
             def _():
                 make(me + d, 0).start()
 
+            if after is not None:
+                after(me + d)
+
         @pl.when(me - d >= 0)
         def _():
             make(me - d, 0).wait_recv()
@@ -110,8 +128,14 @@
             def _():
                 make(me - d, 1).start()
 
-    for part in range(SPLIT):
-        send_own(lambda way, part=part: kv_copy(me * SPLIT + part, way))
+            if after is not None:
+                after(me - d)
+
+    send_own(lambda way: kv_copy(me * xn + xi, way))
+
+    def share(src):
+        for s in range(1, xn):
+            kx_copy(src * xn + xi, s).start()
 
     def absorb(i, _):
         block = q[:, pl.ds(pl.multiple_of(i * pair, pair), pair)]
@@ -146,10 +170,19 @@
     half = heads // 4
     lax.fori_loop(0, half, absorb, 0)
     for d in range(1, n):
-        for part in range(SPLIT):
-            take(lambda src, way, part=part: kv_copy(src * SPLIT + part, way), d)
+        take(lambda src, way: kv_copy(src * xn + xi, way), d, share)
         if d == 1:
             lax.fori_loop(half, heads // 2, absorb, 0)
+
+    def shared(src, _):
+        @pl.when(src != me)
+        def _():
+            for s in range(1, xn):
+                kx_copy(src * xn + lax.rem(xi + s, xn), s).wait_recv()
+
+        return 0
+
+    lax.fori_loop(0, n, shared, 0)
     loads[2].wait()
 
     def attend(m, _):
@@ -157,24 +190,24 @@
         rows = pl.ds(pl.multiple_of(tb * ts, ts), ts)
         unit = me * SPLIT + tb
         all_keys = keys[...].reshape(ctx, keys.shape[2])
-        hide = bias[rows, :]
-        for p in range(hg_heads // 2):
-            h = hg * hg_heads + 2 * p
-            wq = wide[pl.ds(h, 2), rows, :].reshape(2 * ts, wide.shape[2])
+        hide = jnp.concatenate([bias[rows, :]] * batch, axis=0)
+        for p in range(hg_heads // batch):
+            h = hg * hg_heads + batch * p
+            wq = wide[pl.ds(h, batch), rows, :].reshape(batch * ts, wide.shape[2])
             scores = lax.dot_general(
                 wq, all_keys, (((1,), (1,)), ((), ())), preferred_element_type=f32
             )
-            scores = scores * scale + jnp.concatenate([hide, hide], axis=0)
+            scores = scores * scale + hide
             peak = jnp.max(scores, axis=1, keepdims=True)
             weights = jnp.exp2(scores - peak)
             total = jnp.sum(weights, axis=1, keepdims=True)
             mixed = jnp.dot(weights.astype(bf16), all_keys[:, :lat], preferred_element_type=f32)
             mixed = (mixed / total).astype(bf16)
-            for k in range(2):
+            for k in range(batch):
                 value = jnp.dot(
                     mixed[k * ts : (k + 1) * ts], vu[h + k], preferred_element_type=f32
                 )
-                lo = (2 * p + k) * vdim
+                lo = (batch * p + k) * vdim
                 full[unit, hg, :, lo : lo + vdim] = value.astype(bf16)
         send_own(lambda way: z_copy(unit, hg, way))
         return 0
@@ -246,13 +279,30 @@
 
             @pl.when(did)
             def _():
-                kv_copy(unit, way).wait_send()
                 for hg in range(hgs):
                     z_copy(unit, hg, way).wait_send()
 
         return 0
 
     lax.fori_loop(0, units, sent, 0)
+
+    def kv_sent(src, _):
+        @pl.when(has_left & (src >= me))
+        def _():
+            kv_copy(src * xn + xi, 0).wait_send()
+
+        @pl.when(has_right & (src <= me))
+        def _():
+            kv_copy(src * xn + xi, 1).wait_send()
+
+        @pl.when(src != me)
+        def _():
+            for s in range(1, xn):
+                kx_copy(src * xn + xi, s).wait_send()
+
+        return 0
+
+    lax.fori_loop(0, n, kv_sent, 0)
 
     for lu in range(upx):
         for t in range(ntiles):
@@ -289,12 +339,11 @@
     tokens = q_heads.shape[1]
     rope = cache_rope.shape[2]
     rows_all, width = out_weight.shape[1:]
-    keys = jnp.concatenate([cache_latent[0], cache_rope[0], cache_rope[0]], axis=1)
     kw = lat + 2 * rope
     ts = tokens // SPLIT
     units = n * SPLIT
     upx = units // xn
-    hg_heads = math.gcd(8, heads)
+    hg_heads = math.gcd(16, heads)
     hgs = heads // hg_heads
     nt = 256 if width % 256 == 0 else width
     ntiles = width // nt
@@ -306,6 +355,7 @@
         out_shape=jax.ShapeDtypeStruct((upx * ts, width), bf16),
         in_specs=[
             pl.BlockSpec(memory_space=vmem),
+            pl.BlockSpec(memory_space=vmem),
             pl.BlockSpec(memory_space=smem),
             pl.BlockSpec(memory_space=smem),
             hbm,
@@ -315,7 +365,7 @@
         ],
         out_specs=pl.BlockSpec(memory_space=vmem),
         scratch_shapes=[
-            vmem((units, ts, kw), bf16),
+            vmem((n * xn, tokens // xn, kw), bf16),
             vmem(q_heads.shape[1:], bf16),
             vmem(key_up.shape[1:], bf16),
             vmem(value_up.shape[1:], bf16),
@@ -327,8 +377,9 @@
             vmem((units, ntiles, ts, nt), bf16),
             vmem((xn, upx, ntiles, ts, nt), bf16),
             pltpu.SemaphoreType.DMA((4,)),
-            pltpu.SemaphoreType.DMA((2, units)),
-            pltpu.SemaphoreType.DMA((units,)),
+            pltpu.SemaphoreType.DMA((2, n * xn)),
+            pltpu.SemaphoreType.DMA((n * xn,)),
+            pltpu.SemaphoreType.DMA((xn, n * xn)),
             pltpu.SemaphoreType.DMA((2, units, hgs)),
             pltpu.SemaphoreType.DMA((units, hgs)),
             pltpu.SemaphoreType.DMA((units, ntiles)),
@@ -342,7 +393,7 @@
             bytes_accessed=2 * rows_all * width,
             transcendentals=tokens * heads * ctx,
         ),
-    )(keys, span_start, prefix_len, q_heads[0], key_up[0], value_up[0], out_weight[0])
+    )(cache_latent[0], cache_rope[0], span_start, prefix_len, q_heads[0], key_up[0], value_up[0], out_weight[0])
     return out[None]
 
 

time: 100 us -> 113 us (1.13)
  Pallas kernels: 95.1 us -> 110 us
  other arithmetic: 1.66 us -> 0 us
    pallas_call x1, Pallas kernels: 95.1 us -> 110 us  [on_device(): pl.pallas_call(functools.partial(kernel, n, xn), out_shape=jax.ShapeDtype...]
    concatenate x1 -> x0, other arithmetic: 1.66 us -> none  [on_device(): jnp.concatenate([cache_latent[0], cache_rope[0], cache_rope[0]], axis=1)]
where the time goes in v3:
time: 113 us
  Pallas kernels  110 us (97%)
  local copies, waits for them, and re-layouts  3.59 us (3%)
    pallas_call x1, Pallas kernels, on_device(): pl.pallas_call(functools.partial(kernel, n, xn), out_shape=jax.ShapeDtype...  110 us
    unnamed x2, local copies, waits for them, and re-layouts  3.59 us

profile of v3, /device:TPU:0, one launch (start us, length us, event | category | flops | bytes accessed | tf_op | source)
XLA Modules:
  0.0 113.2 jit_solution(1150777195804195644)
XLA Ops:
  0.0 1.4 %copy.9 = bf16[1,128,64]{2,1,0:T(8,128)(2,1)} copy(bf16[1,128,64]{1,2,0:T(8,128)(2,1)} %param.10) | data formatting | bytes 32768 | tf_op args[2]
  1.4 109.6 %shard_map.82 = bf16[256,1792]{1,0:T(8,128)(2,1)} custom-call(bf16[128,512]{1,0:T(8,128)(2,1)} %bitcast.13, bf16[128,64]{1,0:T(8,128)(2,1)} %bitcast.8, s32[1,2]{1,0:T(1,128)} %start_ref.1, s32[1,2]{1,0:T(1,128)} %prefix_ref.1, bf16[128,6144]{1,0:T(8,128)(2,1)} %bitcast.12, bf16[32,128,512]{2,1,0:T(8,128)(2,1)} %bitcast.10, bf16[32,512,128]{2,1,0:T(8,128)(2,1)} %bitcast.11, ...), custom_call_target="tpu_custom_call" | custom-call | flops 12884901888 | bytes 14680064 | tf_op jit(solution)/shard_map/pallas_call | solution.py:353
  111.0 2.2 %copy.11 = bf16[1,256,1792]{2,1,0:T(8,128)(2,1)} copy(bf16[1,256,1792]{2,1,0:T(8,128)(2,1)} %bitcast.7) | data formatting | bytes 1835008

commit v4 on v3

--- a/solution.py
+++ b/solution.py
@@ -9,7 +9,7 @@
 from jax.sharding import PartitionSpec as P
 
 NSPAN = 2
-SPLIT = 4
+SPLIT = 2
 masked_fill = -1e30
 f32, bf16 = jnp.float32, jnp.bfloat16
 
@@ -28,7 +28,7 @@
     rope = pair // 2 - nope
     units, hgs, ts, hw = full.shape
     hg_heads = hw // vdim
-    batch = min(4, hg_heads)
+    batch = 2
     upx, ntiles, _, nt = acc.shape
     ctx = n * tokens
     scale = math.log2(math.e) * (pair // 2) ** (-0.5)
@@ -343,7 +343,7 @@
     ts = tokens // SPLIT
     units = n * SPLIT
     upx = units // xn
-    hg_heads = math.gcd(16, heads)
+    hg_heads = math.gcd(8, heads)
     hgs = heads // hg_heads
     nt = 256 if width % 256 == 0 else width
     ntiles = width // nt

time: 113 us -> 101 us (0.89)
  Pallas kernels: 110 us -> 96.9 us
    pallas_call x1, Pallas kernels: 110 us -> 96.9 us  [on_device(): pl.pallas_call(functools.partial(kernel, n, xn), out_shape=jax.ShapeDtype...]
where the time goes in v4:
time: 101 us; the launch traced here: 100 us
  Pallas kernels  96.9 us (96%)
  local copies, waits for them, and re-layouts  3.59 us (4%)
    pallas_call x1, Pallas kernels, on_device(): pl.pallas_call(functools.partial(kernel, n, xn), out_shape=jax.ShapeDtype...  96.9 us
    unnamed x2, local copies, waits for them, and re-layouts  3.59 us

profile of v4, /device:TPU:0, one launch (start us, length us, event | category | flops | bytes accessed | tf_op | source)
XLA Modules:
  0.0 100.5 jit_solution(17614924028024680562)
XLA Ops:
  0.0 1.4 %copy.9 = bf16[1,128,64]{2,1,0:T(8,128)(2,1)} copy(bf16[1,128,64]{1,2,0:T(8,128)(2,1)} %param.10) | data formatting | bytes 32768 | tf_op args[2]
  1.4 96.9 %shard_map.82 = bf16[256,1792]{1,0:T(8,128)(2,1)} custom-call(bf16[128,512]{1,0:T(8,128)(2,1)} %bitcast.13, bf16[128,64]{1,0:T(8,128)(2,1)} %bitcast.8, s32[1,2]{1,0:T(1,128)} %start_ref.1, s32[1,2]{1,0:T(1,128)} %prefix_ref.1, bf16[128,6144]{1,0:T(8,128)(2,1)} %bitcast.12, bf16[32,128,512]{2,1,0:T(8,128)(2,1)} %bitcast.10, bf16[32,512,128]{2,1,0:T(8,128)(2,1)} %bitcast.11, ...), custom_call_target="tpu_custom_call" | custom-call | flops 12884901888 | bytes 14680064 | tf_op jit(solution)/shard_map/pallas_call | solution.py:353
  98.3 2.2 %copy.11 = bf16[1,256,1792]{2,1,0:T(8,128)(2,1)} copy(bf16[1,256,1792]{2,1,0:T(8,128)(2,1)} %bitcast.7) | data formatting | bytes 1835008
